TPU v7x, 32 devices: a whole 2x2x4 slice. The times are simulated.
32 devices in a mesh: shard: 8 (over y, x, core), ctx: 4 (over z).
Axes of the slice: x: 2, y: 2, z: 4, core: 2. Of those that a mesh axis runs over, the one named last changes fastest.
Arguments:
- embedded: bfloat16 [4096, 8192], P('shard', 'ctx'), may hold values from -6 to 6
- w_query: bfloat16 [8192, 4096], P('shard', 'ctx'), may hold values from -0.0625 to 0.0625
- w_key: bfloat16 [8192, 4096], P('shard', 'ctx'), may hold values from -0.0625 to 0.0625
- w_value: bfloat16 [8192, 4096], P('shard', 'ctx'), may hold values from -0.0625 to 0.0625
- short_taps: float32 [3, 3, 4096], P(None, None, 'ctx'), may hold values from -3 to 3
- long_filter: float32 [128, 256], P(None, 'ctx'), may hold values from -0.5 to 0.5
- skip_gain: float32 [4096], P('ctx'), may hold values from -4 to 4
Outputs:
- gated: bfloat16 [4096, 4096], P('shard', 'ctx')
All inputs are finite; a program needn't handle non-finite values.
Results may differ from a plain program's by a relative error of at most 0.007.
Values may be sent and summed in bfloat16 or wider, within the bound.
A program may use at most 128 MiB of HBM per device.

v0:
```python
import jax
import jax.numpy as jnp
from jax import lax
from jax.sharding import PartitionSpec as P


def shifted(value, axis, steps):
    count = lax.axis_size(axis)
    initial, last = (max(0, -steps), min(count, count - steps))
    return lax.ppermute(value, axis, [(source, source + steps) for source in range(initial, last)])


def short_tail(field_rows, tap_weights, out_count):
    values = field_rows.astype(jnp.float32)
    total_rows = values.shape[0]
    running = tap_weights[0] * values[total_rows - out_count :]
    running = running + tap_weights[1] * values[total_rows - out_count - 1 : total_rows - 1]
    running = running + tap_weights[2] * values[total_rows - out_count - 2 : total_rows - 2]
    return running


def long_conv(mixed_ext, long_filter, row_count):
    tap_count = long_filter.shape[0]
    groups = long_filter.shape[1]
    local_width = mixed_ext.shape[1]
    group_width = local_width // groups
    exact_mode = lax.Precision.HIGHEST
    blocked = mixed_ext.astype(jnp.float32).reshape(
        row_count // tap_count + 1, tap_count, groups, group_width
    )
    lag_grid = lax.broadcasted_iota(jnp.int32, (tap_count, tap_count), 0) - lax.broadcasted_iota(
        jnp.int32, (tap_count, tap_count), 1
    )
    tap_ids = lax.broadcasted_iota(jnp.int32, (tap_count, tap_count, tap_count), 2)
    near_hot = (tap_ids == lag_grid[:, :, None]).astype(jnp.float32)
    far_hot = (tap_ids == (lag_grid + tap_count)[:, :, None]).astype(jnp.float32)
    near_mat = jnp.einsum("tsj,jg->gts", near_hot, long_filter, precision=exact_mode)
    far_mat = jnp.einsum("tsj,jg->gts", far_hot, long_filter, precision=exact_mode)
    filtered = jnp.einsum("gts,bsgc->btgc", near_mat, blocked[1:], precision=exact_mode)
    filtered = filtered + jnp.einsum("gts,bsgc->btgc", far_mat, blocked[:-1], precision=exact_mode)
    return filtered.reshape(row_count, local_width)


def local(embedded, w_query, w_key, w_value, short_taps, long_filter, skip_gain):
    row_count = embedded.shape[0]
    tap_count = long_filter.shape[0]
    local_width = w_query.shape[1]
    gathered = lax.all_gather(embedded, "ctx", axis=1, tiled=True)
    query_rows = jnp.dot(
        gathered,
        lax.all_gather(w_query, "shard", axis=0, tiled=True),
        preferred_element_type=jnp.float32,
    ).astype(jnp.bfloat16)
    key_rows = jnp.dot(
        gathered,
        lax.all_gather(w_key, "shard", axis=0, tiled=True),
        preferred_element_type=jnp.float32,
    ).astype(jnp.bfloat16)
    value_rows = jnp.dot(
        gathered,
        lax.all_gather(w_value, "shard", axis=0, tiled=True),
        preferred_element_type=jnp.float32,
    ).astype(jnp.bfloat16)
    zero_row = jnp.zeros((1, local_width), jnp.bfloat16)
    edge_block = shifted(
        jnp.stack(
            [query_rows[row_count - 2 :], key_rows[row_count - 2 :], value_rows[row_count - 2 :]]
        ),
        "shard",
        1,
    )
    query_short = short_tail(
        jnp.concatenate([edge_block[0], query_rows], axis=0), short_taps[0], row_count
    )
    key_short = short_tail(
        jnp.concatenate([edge_block[1], key_rows], axis=0), short_taps[1], row_count
    )
    value_short = short_tail(
        jnp.concatenate([edge_block[2], value_rows], axis=0), short_taps[2], row_count
    )
    mixed_rows = (key_short * value_short).astype(jnp.bfloat16)
    mixed_edge = shifted(mixed_rows[row_count - tap_count + 1 :], "shard", 1)
    mixed_ext = jnp.concatenate([zero_row, mixed_edge, mixed_rows], axis=0)
    long_out = long_conv(mixed_ext, long_filter, row_count)
    return (query_short * (long_out + skip_gain * mixed_rows.astype(jnp.float32))).astype(
        jnp.bfloat16
    )


def solution(mesh):
    in_specs = (
        P("shard", "ctx"),
        P("shard", "ctx"),
        P("shard", "ctx"),
        P("shard", "ctx"),
        P(None, None, "ctx"),
        P(None, "ctx"),
        P("ctx"),
    )
    out_specs = P("shard", "ctx")
    return jax.shard_map(local, mesh=mesh, in_specs=in_specs, out_specs=out_specs, check_vma=False)
```

profile of v0, /device:TPU:1, one launch (start us, length us, event | category | flops | bytes accessed | tf_op | source)
XLA Modules:
  0.0 507.1 jit_solution(3801923479743798748)
XLA Ops:
  6.5 0.0 copy-start
  6.5 0.0 all-gather.5.cloned.1.call-start
  6.5 0.7 all-gather.5.cloned.1.call-update
  7.3 0.0 all-gather.11.cloned.1.call-start
  7.3 0.7 all-gather.11.cloned.1.call-update
  8.0 0.0 copy-start.3
  8.0 0.0 all-gather.9.cloned.1.call-start
  8.1 0.7 all-gather.9.cloned.1.call-update
  8.8 0.0 all-gather.7.cloned.1.call-start
  8.8 0.5 all-gather.7.cloned.1.call-update
  9.3 0.0 copy-done.3
  9.4 0.0 copy-done
  9.4 7.9 %fusion = f32[128,128,64]{1,2,0:T(8,128)} fusion(s32[128,128]{1,0:T(8,128)S(1)} %iota_subtract_fusion, f32[128,64]{0,1:T(8,128)S(1)} %copy-done), kind=kOutput, calls=%fused_computation.2 | convolution fusion | flops 1612709888 | bytes 4292608 | tf_op jit(solution)/shard_map/tsj,jg->gts/dot_general | solution.py:37
  17.3 143.6 %all-gather.5.cloned.1.call-done = bf16[512,8192]{1,0:T(8,128)(2,1)} async-done(((bf16[512,2048]{1,0:T(8,128)(2,1)}), bf16[512,8192]{1,0:T(8,128)(2,1)}) %all-gather.5.cloned.1.call-update) | async-done | bytes 8388624 | tf_op jit(solution)/shard_map/all_gather | solution.py:48
  160.9 90.2 %all-gather.11.cloned.1.call-done = bf16[8192,1024]{1,0:T(8,128)(2,1)} async-done(((bf16[1024,1024]{1,0:T(8,128)(2,1)}), bf16[8192,1024]{1,0:T(8,128)(2,1)}) %all-gather.11.cloned.1.call-update) | async-done | bytes 16777232 | tf_op jit(solution)/shard_map/all_gather | solution.py:61
  251.1 14.8 %convolution_convert_fusion = bf16[512,1024]{1,0:T(8,128)(2,1)S(1)} fusion(bf16[512,8192]{1,0:T(8,128)(2,1)} %all-gather.5.cloned.1.call-done, bf16[8192,1024]{1,0:T(8,128)(2,1)} %all-gather.11.cloned.1.call-done), kind=kOutput, calls=%fused_computation.33 | convolution fusion | flops 8590458880 | bytes 26214400 | tf_op jit(solution)/shard_map/dot_general | solution.py:59
  265.9 77.0 %all-gather.9.cloned.1.call-done = bf16[8192,1024]{1,0:T(8,128)(2,1)} async-done(((bf16[1024,1024]{1,0:T(8,128)(2,1)}), bf16[8192,1024]{1,0:T(8,128)(2,1)}) %all-gather.9.cloned.1.call-update) | async-done | bytes 16777232 | tf_op jit(solution)/shard_map/all_gather | solution.py:56
  342.9 14.8 %convolution_convert_fusion.1 = bf16[512,1024]{1,0:T(8,128)(2,1)S(1)} fusion(bf16[512,8192]{1,0:T(8,128)(2,1)} %all-gather.5.cloned.1.call-done, bf16[8192,1024]{1,0:T(8,128)(2,1)} %all-gather.9.cloned.1.call-done), kind=kOutput, calls=%fused_computation.34 | convolution fusion | flops 8590458880 | bytes 26214400 | tf_op jit(solution)/shard_map/dot_general | solution.py:54
  357.6 76.9 %all-gather.7.cloned.1.call-done = bf16[8192,1024]{1,0:T(8,128)(2,1)} async-done(((bf16[1024,1024]{1,0:T(8,128)(2,1)}), bf16[8192,1024]{1,0:T(8,128)(2,1)}) %all-gather.7.cloned.1.call-update) | async-done | bytes 16777232 | tf_op jit(solution)/shard_map/all_gather | solution.py:51
  434.5 14.8 %convolution_convert_fusion.2 = bf16[512,1024]{1,0:T(8,128)(2,1)S(1)} fusion(bf16[512,8192]{1,0:T(8,128)(2,1)} %all-gather.5.cloned.1.call-done, bf16[8192,1024]{1,0:T(8,128)(2,1)} %all-gather.7.cloned.1.call-done), kind=kOutput, calls=%fused_computation.35 | convolution fusion | flops 8590458880 | bytes 26214400 | tf_op jit(solution)/shard_map/dot_general | solution.py:49
  449.3 3.2 collective-permute-start
  452.6 0.0 copy-start.4
  452.6 0.8 collective-permute-done
  453.4 0.3 maximum_convert_fusion.2
  453.7 0.6 maximum_convert_fusion
  454.3 0.0 copy-done.4
  454.3 1.3 fusion.12
  455.7 0.8 slice.149
  456.4 4.2 collective-permute-start.1
  460.6 7.9 %fusion.1 = f32[128,128,64]{1,2,0:T(8,128)} fusion(s32[128,128]{1,0:T(8,128)S(1)} %broadcast_add_fusion, f32[128,64]{0,1:T(8,128)S(1)} %copy-done), kind=kOutput, calls=%fused_computation.3 | convolution fusion | flops 1612709888 | bytes 4292608 | tf_op jit(solution)/shard_map/tsj,jg->gts/dot_general | solution.py:38
  468.5 0.0 slice-start
  468.5 1.3 copy.11
  469.8 2.2 slice.130
  472.0 0.0 collective-permute-done.1
  472.0 0.0 slice-done
  472.0 1.2 pad_maximum_fusion
  473.2 2.3 copy.13
  475.5 2.1 slice.133
  477.7 0.0 copy-start.1
  477.7 0.0 copy-start.2
  477.7 8.3 %fusion.2 = f32[64,4,16,128]{3,2,1,0:T(8,128)S(1)} fusion(f32[128,128,64]{1,2,0:T(8,128)} %fusion.1, bf16[4,128,64,16]{1,0,3,2:T(4,128)(2,1)} %slice.133), kind=kOutput, calls=%fused_computation.4 | convolution fusion | flops 805306368 | bytes 7340032 | tf_op jit(solution)/shard_map/gts,bsgc->btgc/dot_general | solution.py:40
  486.0 0.0 copy-done.1
  486.0 0.0 copy-done.2
  486.0 5.7 %add_bitcast_fusion = f32[4,128,64,16]{1,3,0,2:T(8,128)S(1)} fusion(f32[64,4,16,128]{3,2,1,0:T(8,128)S(1)} %fusion.2, f32[128,128,64]{1,2,0:T(8,128)S(1)} %copy-done.1, bf16[4,128,64,16]{1,0,3,2:T(4,128)(2,1)S(1)} %copy-done.2), kind=kOutput, calls=%fused_computation.32 | convolution fusion | flops 805830656 | bytes 9437184 | tf_op jit(solution)/shard_map/gts,bsgc->btgc/dot_general | solution.py:39
  491.7 1.0 copy.15
  492.7 1.5 copy.37
  494.2 0.0 copy-start.5
  494.2 2.9 copy.16
  497.1 0.0 copy-done.5
  497.1 3.5 fusion.18
  (9 shorter events, 0.1 us)
Async XLA Ops:
  6.5 2.9 copy-start
  6.5 154.4 %all-gather.5.cloned.1.call-start = ((), (), s32[]{:S(2)}) async-start(), calls=%async_computation | async-start | bytes 10485760 | tf_op jit(solution)/shard_map/all_gather | solution.py:48
  7.3 243.8 %all-gather.11.cloned.1.call-start = ((), (), s32[]{:S(2)}) async-start(), calls=%async_computation.3 | async-start | bytes 18874368 | tf_op jit(solution)/shard_map/all_gather | solution.py:61
  8.0 1.3 copy-start.3
  8.0 334.8 %all-gather.9.cloned.1.call-start = ((), (), s32[]{:S(2)}) async-start(), calls=%async_computation.2 | async-start | bytes 18874368 | tf_op jit(solution)/shard_map/all_gather | solution.py:56
  8.8 425.7 %all-gather.7.cloned.1.call-start = ((), (), s32[]{:S(2)}) async-start(), calls=%async_computation.1 | async-start | bytes 18874368 | tf_op jit(solution)/shard_map/all_gather | solution.py:51
  449.3 4.0 collective-permute-start
  452.6 1.7 copy-start.4
  456.4 15.6 %collective-permute-start.1 = (bf16[127,1024]{1,0:T(8,128)(2,1)}, bf16[127,1024]{1,0:T(8,128)(2,1)S(1)}, u32[]{:S(2)}, u32[]{:S(2)}) collective-permute-start(bf16[127,1024]{1,0:T(8,128)(2,1)} %slice.149), channel_id=1, source_target_pairs={{0,4},{4,8},{8,12},{12,16},{16,20},{20,24},{24,28},{1,5},{5,9},{9,... | collective-permute-start | bytes 780296 | tf_op jit(solution)/shard_map/ppermute | solution.py:10
  468.5 3.5 slice-start
  477.7 8.3 %copy-start.1 = (f32[128,128,64]{1,2,0:T(8,128)S(1)}, f32[128,128,64]{1,2,0:T(8,128)}, u32[]{:S(2)}) copy-start(f32[128,128,64]{1,2,0:T(8,128)} %fusion) | copy-start | bytes 12582916
  477.7 8.3 %copy-start.2 = (bf16[4,128,64,16]{1,0,3,2:T(4,128)(2,1)S(1)}, bf16[4,128,64,16]{1,0,3,2:T(4,128)(2,1)}, u32[]{:S(2)}) copy-start(bf16[4,128,64,16]{1,0,3,2:T(4,128)(2,1)} %slice.130) | copy-start | bytes 3145732
  494.2 2.9 copy-start.5
Sparse Core Ops, SparseCore 0:
  8.9 151.9 all-gather.4
  162.8 88.2 all-gather.10
  253.0 89.8 all-gather.8
  344.6 89.8 all-gather.6
where the time goes:
time: 507 us
  waiting for transfers between devices  391 us (77%)
  matrix products  74.1 us (15%)
  local copies, waits for them, and re-layouts  14.2 us (3%)
  between operations  13.3 us (3%)
  starting transfers between devices  7.53 us (1%)
  other arithmetic  6.99 us (1%)
    all_gather x1, waiting for transfers between devices, local(): gathered = lax.all_gather(embedded, 'ctx', axis=1, tiled=True)  144 us
    all_gather x1, waiting for transfers between devices, local(): lax.all_gather(w_value, 'shard', axis=0, tiled=True)  90.2 us
    all_gather x1, waiting for transfers between devices, local(): lax.all_gather(w_key, 'shard', axis=0, tiled=True)  77 us
    all_gather x1, waiting for transfers between devices, local(): lax.all_gather(w_query, 'shard', axis=0, tiled=True)  76.9 us
    dot_general x1, matrix products, local(): jnp.dot(gathered, lax.all_gather(w_value, 'shard', axis=0, tiled=True), p...  14.8 us
    dot_general x1, matrix products, local(): jnp.dot(gathered, lax.all_gather(w_key, 'shard', axis=0, tiled=True), pre...  14.8 us
    dot_general x1, matrix products, local(): jnp.dot(gathered, lax.all_gather(w_query, 'shard', axis=0, tiled=True), p...  14.8 us
  transfers between devices with their start and end apart: 6, of which 5 were waited for; matrix products, arithmetic and copies ran while one was open for 10% of the time, Pallas kernels for 0%

commit v1 on v0

v1 whole, which is shorter than its diff:
```python
import functools

import jax
import jax.numpy as jnp
from jax import lax
from jax.experimental import pallas as pl
from jax.experimental.pallas import tpu as pltpu
from jax.sharding import PartitionSpec as P

CHUNKS = 4
HALVES = 2
PIECES = 4
AHEAD = 2
TILE = 256
MESH = pl.DeviceIdType.MESH


def forward(value, axis, steps):
    count = lax.axis_size(axis)
    return lax.ppermute(value, axis, [(source, source + steps) for source in range(count - steps)])


def projection_kernel(
    names, embedded, w_key, w_value, w_query, out,
    wbuf, ebuf, gbuf, osend, orecv, acc,
    wy_sem, wc_sem, wo_sem, zs_sem, zr_sem, x_sem, o_sem, local_sem,
):
    shards, blocks = lax.axis_size(names[0]), lax.axis_size(names[1])
    per = shards // blocks
    groups = blocks // 2
    place, z = lax.axis_index(names[0]), lax.axis_index(names[1])
    core = place % per
    side = (place // per) % 2
    group = place // (2 * per)
    weights = (w_key, w_value, w_query)
    rows, wide = embedded.shape
    depth, width = w_key.shape
    piece = rows // CHUNKS
    half = rows // HALVES
    cut = depth // PIECES
    core_place = place + 1 - 2 * core
    side_place = place + per * (1 - 2 * side)

    def group_place(step):
        return lax.rem(group + step, groups) * 2 * per + side * per + core

    def remote(src, dst, send, recv, where):
        return pltpu.make_async_remote_copy(
            src_ref=src, dst_ref=dst, send_sem=send, recv_sem=recv,
            device_id=where, device_id_type=MESH,
        )

    def either(body, *conditions):
        flag = conditions[0]
        for other in conditions[1:]:
            flag = jnp.logical_and(flag, other)
        pl.when(flag)(body)

    barrier = pltpu.get_barrier_semaphore()
    partners = [core_place, side_place] + [group_place(j) for j in range(1, groups)]
    for partner in partners:
        pl.semaphore_signal(barrier, inc=1, device_id=(partner, z), device_id_type=MESH)

    @pl.when(z > 0)
    def _():
        pl.semaphore_signal(barrier, inc=1, device_id=(place, z - 1), device_id_type=MESH)

    @pl.when(z < blocks - 1)
    def _():
        pl.semaphore_signal(barrier, inc=1, device_id=(place, z + 1), device_id_type=MESH)

    ends = jnp.where(z > 0, 1, 0) + jnp.where(z < blocks - 1, 1, 0)
    pl.semaphore_wait(barrier, len(partners) + ends)

    def chunk(c):
        return pl.ds(c * piece, piece)

    def own_rows(k):
        return pl.ds(pl.multiple_of(core * depth + k * cut, 16), cut)

    pieces = [(p, j, k) for p in range(3) for j in range(1, groups) for k in range(PIECES)]

    def w_across(q):
        p, j, k = pieces[q]
        return remote(
            weights[p].at[pl.ds(k * cut, cut)], wbuf.at[p, j, own_rows(k)],
            wy_sem.at[0, q], wy_sem.at[1, q], (group_place(groups - j), z),
        )

    def w_core(q):
        p, j, k = pieces[q]
        ref = wbuf.at[p, j, own_rows(k)]
        return remote(ref, ref, wc_sem.at[0, q], wc_sem.at[1, q], (core_place, z))

    def w_own(p):
        mine = pl.ds(pl.multiple_of(core * depth, 16), depth)
        return remote(
            weights[p], wbuf.at[p, 0, mine], wo_sem.at[0, p], wo_sem.at[1, p], (core_place, z)
        )

    def w_here(p):
        mine = pl.ds(pl.multiple_of(core * depth, 16), depth)
        return pltpu.make_async_copy(weights[p], wbuf.at[p, 0, mine], local_sem.at[p])

    def up(c, r):
        src = embedded.at[chunk(c)] if r == 1 else ebuf.at[z - (r - 1), chunk(c)]
        return remote(
            src, ebuf.at[z - (r - 1), chunk(c)], zs_sem.at[0, c, r - 1], zr_sem.at[0, c, r - 1],
            (place, z + 1),
        )

    def down(c, r):
        src = embedded.at[chunk(c)] if r == 1 else ebuf.at[z + (r - 1), chunk(c)]
        return remote(
            src, ebuf.at[z + (r - 1), chunk(c)], zs_sem.at[1, c, r - 1], zr_sem.at[1, c, r - 1],
            (place, z - 1),
        )

    def across(c, f, src):
        return remote(
            src, gbuf.at[f // 2, chunk(c)], x_sem.at[0, c, f // 2], x_sem.at[1, c, f // 2],
            (side_place, z),
        )

    def own_embedded(c):
        either(lambda: up(c, 1).start(), z < blocks - 1)
        either(lambda: down(c, 1).start(), z > 0)
        either(lambda: across(c, z, embedded.at[chunk(c)]).start(), z % 2 != side)

    def step(c, r):
        @pl.when(z >= r)
        def _():
            f = z - r
            pltpu.make_async_copy(
                ebuf.at[f, chunk(c)], ebuf.at[f, chunk(c)], zr_sem.at[0, c, r - 1]
            ).wait()
            if r < blocks - 1:
                either(lambda: up(c, r + 1).start(), z < blocks - 1)
            either(lambda: across(c, f, ebuf.at[f, chunk(c)]).start(), f % 2 != side)

        @pl.when(z + r < blocks)
        def _():
            f = z + r
            pltpu.make_async_copy(
                ebuf.at[f, chunk(c)], ebuf.at[f, chunk(c)], zr_sem.at[1, c, r - 1]
            ).wait()
            if r < blocks - 1:
                either(lambda: down(c, r + 1).start(), z > 0)
            either(lambda: across(c, f, ebuf.at[f, chunk(c)]).start(), f % 2 != side)

    def product(p, h, lhs, store):
        at = pl.ds(h * half, half)

        def tile(n, carry):
            cols = pl.ds(pl.multiple_of(n * TILE, TILE), TILE)
            total = None
            for j in range(groups):
                term = jnp.dot(
                    lhs(j)[at, :], wbuf[p, j, :, cols], preferred_element_type=jnp.float32
                )
                total = term if total is None else total + term
            store(at, cols, total)
            return carry

        lax.fori_loop(0, width // TILE, tile, 0)

    def o_copy(p, h):
        at = pl.ds(h * half, half)
        return remote(
            osend.at[p, at], orecv.at[p, at], o_sem.at[0, p, h], o_sem.at[1, p, h], (side_place, z)
        )

    def give(p, h):
        def store(at, cols, total):
            osend[p, at, cols] = total.astype(jnp.bfloat16)

        product(p, h, lambda j: gbuf.at[lax.rem(group + j, groups)], store)
        o_copy(p, h).start()

    def keep(p, h):
        def store(at, cols, total):
            acc[p, at, cols] = total

        product(p, h, lambda j: ebuf.at[2 * lax.rem(group + j, groups) + side], store)

    def finish(p, h):
        at = pl.ds(h * half, half)
        o_copy(p, h).wait_recv()
        out[p, at, :] = (acc[p, at, :] + orecv[p, at, :].astype(jnp.float32)).astype(jnp.bfloat16)

    here = pltpu.make_async_copy(embedded, ebuf.at[z], local_sem.at[3])
    own_embedded(0)
    for q in range(min(AHEAD, len(pieces))):
        w_across(q).start()
    own_embedded(1)
    here.start()
    for p in range(3):
        w_here(p).start()
        w_own(p).start()
    here.wait()
    for p in range(3):
        w_here(p).wait()

    steps = CHUNKS * (blocks - 1)
    weight_ready, rows_ready = {}, {}
    done_pieces = 0
    waited_rows, waited_weights, finished = set(), set(), set()
    pending = [(p, h) for h in range(HALVES) for p in range(3)]
    kept = []

    def ready_rows(h):
        if h in waited_rows:
            return
        waited_rows.add(h)
        for c in range(h * CHUNKS // HALVES, (h + 1) * CHUNKS // HALVES):
            for g in range(groups):
                pltpu.make_async_copy(
                    gbuf.at[g, chunk(c)], gbuf.at[g, chunk(c)], x_sem.at[1, c, g]
                ).wait()

    def ready_weight(p):
        if p in waited_weights:
            return
        waited_weights.add(p)
        w_own(p).wait_recv()
        for q, (owner, _, _) in enumerate(pieces):
            if owner == p:
                w_core(q).wait_recv()

    t = 0
    for c in range(CHUNKS):
        for r in range(1, blocks):
            step(c, r)
            if r == 1 and c + 2 < CHUNKS:
                own_embedded(c + 2)
            while done_pieces < (t + 1) * len(pieces) // steps:
                w_across(done_pieces).wait_recv()
                w_core(done_pieces).start()
                if done_pieces + AHEAD < len(pieces):
                    w_across(done_pieces + AHEAD).start()
                done_pieces += 1
            chunks_in = c if r < blocks - 1 else c + 1
            last = t == steps - 1
            whole = [
                p for p in range(3)
                if done_pieces - (0 if last else 1) >= (p + 1) * (len(pieces) // 3)
            ]
            now = [
                (p, h) for p, h in pending
                if p in whole and (h + 1) * CHUNKS // HALVES <= (chunks_in if last else c)
            ]
            for p, h in now:
                pending.remove((p, h))
                ready_rows(h)
                ready_weight(p)
                give(p, h)
                if last:
                    kept.append((p, h))
                else:
                    keep(p, h)
            t += 1
    for p, h in kept:
        keep(p, h)
    for h in range(HALVES):
        for p in range(3):
            finish(p, h)

    for q in range(len(pieces)):
        w_across(q).wait_send()
        w_core(q).wait_send()
    for p in range(3):
        w_own(p).wait_send()
        for h in range(HALVES):
            o_copy(p, h).wait_send()
    for c in range(CHUNKS):
        for g in range(groups):
            pltpu.make_async_copy(
                gbuf.at[g, chunk(c)], gbuf.at[g, chunk(c)], x_sem.at[0, c, g]
            ).wait()
        for r in range(1, blocks):
            either(lambda: up(c, r).wait_send(), z < blocks - 1, z >= r - 1)
            either(lambda: down(c, r).wait_send(), z > 0, z + r - 1 < blocks)


def project(embedded, w_key, w_value, w_query):
    shards, blocks = lax.axis_size("shard"), lax.axis_size("ctx")
    groups = blocks // 2
    rows, wide = embedded.shape
    depth, width = w_key.shape
    pieces = 3 * (groups - 1) * PIECES
    bf16 = jnp.bfloat16
    dma = pltpu.SemaphoreType.DMA
    flops = 2 * 2 * rows * groups * wide * width * 3
    return pl.pallas_call(
        functools.partial(projection_kernel, ("shard", "ctx")),
        out_shape=jax.ShapeDtypeStruct((3, rows, width), bf16),
        in_specs=[pl.BlockSpec(memory_space=pl.ANY)] * 4,
        out_specs=pl.BlockSpec(memory_space=pltpu.VMEM),
        scratch_shapes=[
            pltpu.VMEM((3, groups, wide, width), bf16),
            pltpu.VMEM((blocks, rows, wide), bf16),
            pltpu.VMEM((groups, rows, wide), bf16),
            pltpu.VMEM((3, rows, width), bf16),
            pltpu.VMEM((3, rows, width), bf16),
            pltpu.VMEM((3, rows, width), jnp.float32),
            dma((2, pieces)),
            dma((2, pieces)),
            dma((2, 3)),
            dma((2, CHUNKS, blocks - 1)),
            dma((2, CHUNKS, blocks - 1)),
            dma((2, CHUNKS, groups)),
            dma((2, 3, HALVES)),
            dma((4,)),
        ],
        compiler_params=pltpu.CompilerParams(
            collective_id=0, has_side_effects=True, vmem_limit_bytes=60 * 1024 * 1024
        ),
        cost_estimate=pl.CostEstimate(
            flops=flops, bytes_accessed=64 * 1024 * 1024, transcendentals=0
        ),
    )(embedded, w_key, w_value, w_query)


def short_conv(ext, taps):
    values = ext.astype(jnp.float32)
    rows = values.shape[0] - 2
    return taps[0] * values[2:] + taps[1] * values[1 : rows + 1] + taps[2] * values[:rows]


def toeplitz(long_filter):
    tap_count = long_filter.shape[0]
    lag = (
        lax.broadcasted_iota(jnp.int32, (tap_count, 2 * tap_count), 0)
        + tap_count
        - lax.broadcasted_iota(jnp.int32, (tap_count, 2 * tap_count), 1)
    )
    hot = (lag[:, :, None] == lax.broadcasted_iota(jnp.int32, (1, 1, tap_count), 2)).astype(
        jnp.bfloat16
    )
    return jnp.einsum(
        "tsj,jg->gts",
        hot,
        long_filter.astype(jnp.bfloat16),
        preferred_element_type=jnp.float32,
    ).astype(jnp.bfloat16)


def long_conv(ext, matrix, row_count):
    groups, tap_count, _ = matrix.shape
    width = ext.shape[1]
    blocks = row_count // tap_count
    cut = ext.reshape(blocks + 1, tap_count, groups, width // groups)
    pair = jnp.concatenate([cut[:-1], cut[1:]], axis=1)
    out = jnp.einsum("gts,bsgc->btgc", matrix, pair, preferred_element_type=jnp.float32)
    return out.reshape(row_count, width)


def local(embedded, w_query, w_key, w_value, short_taps, long_filter, skip_gain):
    row_count = embedded.shape[0]
    tap_count = long_filter.shape[0]
    matrix = toeplitz(long_filter)
    key_rows, value_rows, query_rows = project(embedded, w_key, w_value, w_query)

    key_end, value_end = key_rows[-tap_count - 2 :], value_rows[-tap_count - 2 :]
    mixed_end = (short_conv(key_end, short_taps[1]) * short_conv(value_end, short_taps[2])).astype(
        jnp.bfloat16
    )
    edge = forward(
        jnp.concatenate([mixed_end, query_rows[-2:], key_rows[-2:], value_rows[-2:]], axis=0),
        "shard",
        1,
    )
    query_edge, key_edge, value_edge = [
        edge[tap_count + 2 * p : tap_count + 2 * p + 2] for p in range(3)
    ]
    query_short = short_conv(jnp.concatenate([query_edge, query_rows], axis=0), short_taps[0])
    key_short = short_conv(jnp.concatenate([key_edge, key_rows], axis=0), short_taps[1])
    value_short = short_conv(jnp.concatenate([value_edge, value_rows], axis=0), short_taps[2])
    mixed = (key_short * value_short).astype(jnp.bfloat16)
    long_out = long_conv(jnp.concatenate([edge[:tap_count], mixed], axis=0), matrix, row_count)
    return (query_short * (long_out + skip_gain * mixed.astype(jnp.float32))).astype(jnp.bfloat16)


def solution(mesh):
    in_specs = (
        P("shard", "ctx"),
        P("shard", "ctx"),
        P("shard", "ctx"),
        P("shard", "ctx"),
        P(None, None, "ctx"),
        P(None, "ctx"),
        P("ctx"),
    )
    return jax.shard_map(
        local, mesh=mesh, in_specs=in_specs, out_specs=P("shard", "ctx"), check_vma=False
    )
```

time: 507 us -> 267 us (0.53)
  waiting for transfers between devices: 391 us -> 0.01 us
  Pallas kernels: 0 us -> 218 us
  matrix products: 74.1 us -> 14 us
  between operations: 13.3 us -> 0.17 us
    all_gather x4 -> x0, waiting for transfers between devices: 388 us -> none  [the longest x1 144 us: local(): gathered = lax.all_gather(embedded, 'ctx', axis=1, tiled=True)]
    pallas_call x0 -> x1, Pallas kernels: none -> 218 us  [project(): pl.pallas_call(functools.partial(projection_kernel, ('shard', 'ctx')), ou...]
    dot_general x7 -> x2, matrix products: 74.1 us -> 14 us  [the longest x1 9.13 us: toeplitz(): jnp.einsum('tsj,jg->gts', hot, long_filter.astype(jnp.bfloat16), preferre...]
    slice x7 -> x9, local copies, waits for them, and re-layouts: 7.42 us -> 11.5 us  [the longest x5 10.6 us: long_conv(): pair = jnp.concatenate([cut[:-1], cut[1:]], axis=1)]
  transfers between devices with their start and end apart: 6 -> 1, of which waited for: 5 -> 0; matrix products, arithmetic and copies ran while one was open for 10% -> 4% of each run, Pallas kernels for 0% -> 0%
where the time goes in v1:
time: 267 us; the launch traced here: 266 us
  Pallas kernels  218 us (82%)
  local copies, waits for them, and re-layouts  18.5 us (7%)
  matrix products  14 us (5%)
  other arithmetic  8.44 us (3%)
  starting transfers between devices  7.66 us (3%)
    pallas_call x1, Pallas kernels, project(): pl.pallas_call(functools.partial(projection_kernel, ('shard', 'ctx')), ou...  218 us
    slice x5, local copies, waits for them, and re-layouts, long_conv(): pair = jnp.concatenate([cut[:-1], cut[1:]], axis=1)  10.6 us
    dot_general x1, matrix products, toeplitz(): jnp.einsum('tsj,jg->gts', hot, long_filter.astype(jnp.bfloat16), preferre...  9.13 us
    ppermute x1, starting transfers between devices, forward(): lax.ppermute(value, axis, [(source, source + steps) for source in range(c...  7.66 us
  transfers between devices with their start and end apart: 1, of which 0 were waited for; matrix products, arithmetic and copies ran while one was open for 4% of the time, Pallas kernels for 0%

profile of v1, /device:TPU:1, one launch (start us, length us, event | category | flops | bytes accessed | tf_op | source)
XLA Modules:
  0.0 266.5 jit_solution(4665958736264183620)
XLA Ops:
  0.0 0.0 copy-start.2
  0.0 217.7 %shard_map.73 = bf16[3,512,1024]{2,1,0:T(8,128)(2,1)} custom-call(bf16[512,2048]{1,0:T(8,128)(2,1)} %embedded.1, bf16[1024,1024]{1,0:T(8,128)(2,1)} %w_key.1, bf16[1024,1024]{1,0:T(8,128)(2,1)} %w_value.1, bf16[1024,1024]{1,0:T(8,128)(2,1)} %w_query.1), custom_call_target="tpu_custom_call" | custom-call | flops 25769803776 | bytes 67108864 | tf_op jit(solution)/shard_map/pallas_call | solution.py:294
  217.7 0.8 slice_bitcast_fusion.11
  218.5 1.2 slice_convert_fusion.1
  219.7 0.0 copy-done.2
  219.7 0.0 copy-start.4
  219.7 0.3 fusion.26
  220.1 7.7 %collective-permute-start = (bf16[134,1024]{1,0:T(8,128)(2,1)S(1)}, bf16[134,1024]{1,0:T(8,128)(2,1)S(1)}, u32[]{:S(2)}, u32[]{:S(2)}) collective-permute-start(bf16[134,1024]{1,0:T(8,128)(2,1)S(1)} %pad_maximum_fusion.1), channel_id=1, source_target_pairs={{0,4},{4,8},{8,12},{12,16},{16,20},{20,24},{24,28},{1,5},{5,9},{9,... | collective-permute-start | bytes 823304 | tf_op jit(solution)/shard_map/ppermute | solution.py:20
  227.8 0.1 iota_subtract_fusion
  227.9 0.0 copy-done.4
  227.9 0.0 copy-start
  227.9 9.1 %fusion = bf16[128,256,64]{1,2,0:T(8,128)(2,1)} fusion(s32[128,256]{1,0:T(8,128)S(1)} %iota_subtract_fusion, f32[128,64]{0,1:T(8,128)S(1)} %copy-done.4), kind=kOutput, calls=%fused_computation.1 | convolution fusion | flops 541073408 | bytes 4358144 | tf_op jit(solution)/shard_map/tsj,jg->gts/dot_general | solution.py:340
  237.0 0.0 copy-done
  237.0 0.3 slice_bitcast_fusion.1
  237.3 0.0 collective-permute-done
  237.4 0.3 maximum_convert_fusion.2
  237.7 0.6 maximum_convert_fusion
  238.3 1.3 fusion.7
  239.6 1.3 copy.12
  241.0 1.1 pad_maximum_fusion
  242.1 2.3 copy.11
  244.3 2.2 slice.215
  246.5 2.5 copy.13
  249.0 2.2 slice.216
  251.1 0.0 copy-start.1
  251.1 1.6 copy.14
  252.7 0.0 copy-done.1
  252.7 4.9 %fusion.18 = f32[4,128,64,16]{1,3,0,2:T(8,128)S(1)} fusion(bf16[128,256,64]{1,2,0:T(8,128)(2,1)} %fusion, bf16[4,128,64,16]{1,3,0,2:T(8,128)(2,1)S(1)} %copy.14, bf16[4,128,64,16]{1,3,0,2:T(8,128)(2,1)S(1)} %copy-done.1), kind=kOutput, calls=%fused_computation.29 | convolution fusion | flops 272629760 | bytes 8388608 | tf_op jit(solution)/shard_map/gts,bsgc->btgc/dot_general | solution.py:354
  257.6 1.0 copy.15
  258.6 1.5 copy.27
  260.1 0.0 copy-start.3
  260.1 2.9 %copy.16 = f32[512,1024]{1,0:T(8,128)} copy(f32[512,1024]{0,1:T(8,128)} %bitcast.93) | data formatting | bytes 4194304 | tf_op jit(solution)/shard_map/reshape | solution.py:355
  263.0 0.0 copy-done.3
  263.0 3.5 %fusion.13 = bf16[512,1024]{1,0:T(8,128)(2,1)} fusion(f32[514,1024]{1,0:T(8,128)S(1)} %get-tuple-element.25, f32[512,1024]{1,0:T(8,128)} %copy.16, bf16[512,1024]{1,0:T(8,128)(2,1)S(1)} %fusion.7, f32[1024]{0:T(1024)S(1)} %copy-done.3, f32[1024]{0:T(1024)S(1)} %bitcast.107, f32[1024]{0:T(1024)S(1)} %bitcast.108, f32[1024]{0:T(1024)S(1)} %bitcast.106), kind=kLoop, calls=%fused_computation.22 | loop fusion | flops 5242880 | bytes 10502144 | tf_op jit(solution)/shard_map/convert_element_type | solution.py:381
  (5 shorter events, 0.1 us)
Async XLA Ops:
  0.0 219.7 %copy-start.2 = (f32[3,3,1024]{2,1,0:T(4,128)S(1)}, f32[3,3,1024]{2,1,0:T(4,128)}, u32[]{:S(2)}) copy-start(f32[3,3,1024]{2,1,0:T(4,128)} %param.11) | copy-start | bytes 110596
  219.7 8.2 %copy-start.4 = (f32[128,64]{0,1:T(8,128)S(1)}, f32[128,64]{0,1:T(8,128)}, u32[]{:S(2)}) copy-start(f32[128,64]{0,1:T(8,128)} %param.12) | copy-start | bytes 98308
  220.1 17.2 %collective-permute-start = (bf16[134,1024]{1,0:T(8,128)(2,1)S(1)}, bf16[134,1024]{1,0:T(8,128)(2,1)S(1)}, u32[]{:S(2)}, u32[]{:S(2)}) collective-permute-start(bf16[134,1024]{1,0:T(8,128)(2,1)S(1)} %pad_maximum_fusion.1), channel_id=1, source_target_pairs={{0,4},{4,8},{8,12},{12,16},{16,20},{20,24},{24,28},{1,5},{5,9},{9,... | collective-permute-start | bytes 823304 | tf_op jit(solution)/shard_map/ppermute | solution.py:20
  227.9 9.1 %copy-start = (bf16[3,512,1024]{2,1,0:T(8,128)(2,1)S(1)}, bf16[3,512,1024]{2,1,0:T(8,128)(2,1)}, u32[]{:S(2)}) copy-start(bf16[3,512,1024]{2,1,0:T(8,128)(2,1)} %shard_map.73) | copy-start | bytes 9437188
  251.1 1.6 copy-start.1
  260.1 2.9 %copy-start.3 = (f32[1024]{0:T(1024)S(1)}, f32[1024]{0:T(1024)}, u32[]{:S(2)}) copy-start(f32[1024]{0:T(1024)} %param.13) | copy-start | bytes 12292

commit v2 on v1

--- a/solution.py
+++ b/solution.py
@@ -7,10 +7,10 @@
 from jax.experimental.pallas import tpu as pltpu
 from jax.sharding import PartitionSpec as P
 
-CHUNKS = 4
+CHUNKS = 8
 HALVES = 2
-PIECES = 4
-AHEAD = 2
+PIECES = 8
+AHEAD = 3
 TILE = 256
 MESH = pl.DeviceIdType.MESH
 

time: 267 us -> 251 us (0.940)
  Pallas kernels: 218 us -> 202 us
    pallas_call x1, Pallas kernels: 218 us -> 202 us  [project(): pl.pallas_call(functools.partial(projection_kernel, ('shard', 'ctx')), ou...]
where the time goes in v2:
time: 251 us
  Pallas kernels  202 us (80%)
  local copies, waits for them, and re-layouts  18.5 us (7%)
  matrix products  14 us (6%)
  other arithmetic  8.44 us (3%)
  starting transfers between devices  7.7 us (3%)
    pallas_call x1, Pallas kernels, project(): pl.pallas_call(functools.partial(projection_kernel, ('shard', 'ctx')), ou...  202 us
    slice x5, local copies, waits for them, and re-layouts, long_conv(): pair = jnp.concatenate([cut[:-1], cut[1:]], axis=1)  10.6 us
    dot_general x1, matrix products, toeplitz(): jnp.einsum('tsj,jg->gts', hot, long_filter.astype(jnp.bfloat16), preferre...  9.13 us
    ppermute x1, starting transfers between devices, forward(): lax.ppermute(value, axis, [(source, source + steps) for source in range(c...  7.7 us
  transfers between devices with their start and end apart: 1, of which 0 were waited for; matrix products, arithmetic and copies ran while one was open for 4% of the time, Pallas kernels for 0%

profile of v2, /device:TPU:1, one launch (start us, length us, event | category | flops | bytes accessed | tf_op | source)
XLA Modules:
  0.0 250.7 jit_solution(4825463711147012463)
XLA Ops:
  0.0 0.0 copy-start.2
  0.0 201.9 %shard_map.73 = bf16[3,512,1024]{2,1,0:T(8,128)(2,1)} custom-call(bf16[512,2048]{1,0:T(8,128)(2,1)} %embedded.1, bf16[1024,1024]{1,0:T(8,128)(2,1)} %w_key.1, bf16[1024,1024]{1,0:T(8,128)(2,1)} %w_value.1, bf16[1024,1024]{1,0:T(8,128)(2,1)} %w_query.1), custom_call_target="tpu_custom_call" | custom-call | flops 25769803776 | bytes 67108864 | tf_op jit(solution)/shard_map/pallas_call | solution.py:294
  201.9 0.8 slice_bitcast_fusion.11
  202.7 1.2 slice_convert_fusion.1
  203.9 0.0 copy-done.2
  203.9 0.0 copy-start.4
  203.9 0.3 fusion.26
  204.3 7.7 %collective-permute-start = (bf16[134,1024]{1,0:T(8,128)(2,1)S(1)}, bf16[134,1024]{1,0:T(8,128)(2,1)S(1)}, u32[]{:S(2)}, u32[]{:S(2)}) collective-permute-start(bf16[134,1024]{1,0:T(8,128)(2,1)S(1)} %pad_maximum_fusion.1), channel_id=1, source_target_pairs={{0,4},{4,8},{8,12},{12,16},{16,20},{20,24},{24,28},{1,5},{5,9},{9,... | collective-permute-start | bytes 823304 | tf_op jit(solution)/shard_map/ppermute | solution.py:20
  212.0 0.1 iota_subtract_fusion
  212.1 0.0 copy-done.4
  212.1 0.0 copy-start
  212.1 9.1 %fusion = bf16[128,256,64]{1,2,0:T(8,128)(2,1)} fusion(s32[128,256]{1,0:T(8,128)S(1)} %iota_subtract_fusion, f32[128,64]{0,1:T(8,128)S(1)} %copy-done.4), kind=kOutput, calls=%fused_computation.1 | convolution fusion | flops 541073408 | bytes 4358144 | tf_op jit(solution)/shard_map/tsj,jg->gts/dot_general | solution.py:340
  221.3 0.0 copy-done
  221.3 0.3 slice_bitcast_fusion.1
  221.6 0.0 collective-permute-done
  221.6 0.3 maximum_convert_fusion.2
  221.9 0.6 maximum_convert_fusion
  222.5 1.3 fusion.7
  223.9 1.3 copy.12
  225.2 1.1 pad_maximum_fusion
  226.3 2.3 copy.11
  228.6 2.2 slice.215
  230.7 2.5 copy.13
  233.2 2.2 slice.216
  235.3 0.0 copy-start.1
  235.3 1.6 copy.14
  236.9 0.0 copy-done.1
  236.9 4.9 %fusion.18 = f32[4,128,64,16]{1,3,0,2:T(8,128)S(1)} fusion(bf16[128,256,64]{1,2,0:T(8,128)(2,1)} %fusion, bf16[4,128,64,16]{1,3,0,2:T(8,128)(2,1)S(1)} %copy.14, bf16[4,128,64,16]{1,3,0,2:T(8,128)(2,1)S(1)} %copy-done.1), kind=kOutput, calls=%fused_computation.29 | convolution fusion | flops 272629760 | bytes 8388608 | tf_op jit(solution)/shard_map/gts,bsgc->btgc/dot_general | solution.py:354
  241.8 1.0 copy.15
  242.8 1.5 copy.27
  244.3 0.0 copy-start.3
  244.3 2.9 %copy.16 = f32[512,1024]{1,0:T(8,128)} copy(f32[512,1024]{0,1:T(8,128)} %bitcast.93) | data formatting | bytes 4194304 | tf_op jit(solution)/shard_map/reshape | solution.py:355
  247.2 0.0 copy-done.3
  247.2 3.5 %fusion.13 = bf16[512,1024]{1,0:T(8,128)(2,1)} fusion(f32[514,1024]{1,0:T(8,128)S(1)} %get-tuple-element.25, f32[512,1024]{1,0:T(8,128)} %copy.16, bf16[512,1024]{1,0:T(8,128)(2,1)S(1)} %fusion.7, f32[1024]{0:T(1024)S(1)} %copy-done.3, f32[1024]{0:T(1024)S(1)} %bitcast.107, f32[1024]{0:T(1024)S(1)} %bitcast.108, f32[1024]{0:T(1024)S(1)} %bitcast.106), kind=kLoop, calls=%fused_computation.22 | loop fusion | flops 5242880 | bytes 10502144 | tf_op jit(solution)/shard_map/convert_element_type | solution.py:381
  (5 shorter events, 0.1 us)
Async XLA Ops:
  0.0 203.9 %copy-start.2 = (f32[3,3,1024]{2,1,0:T(4,128)S(1)}, f32[3,3,1024]{2,1,0:T(4,128)}, u32[]{:S(2)}) copy-start(f32[3,3,1024]{2,1,0:T(4,128)} %param.11) | copy-start | bytes 110596
  203.9 8.2 %copy-start.4 = (f32[128,64]{0,1:T(8,128)S(1)}, f32[128,64]{0,1:T(8,128)}, u32[]{:S(2)}) copy-start(f32[128,64]{0,1:T(8,128)} %param.12) | copy-start | bytes 98308
  204.3 17.3 %collective-permute-start = (bf16[134,1024]{1,0:T(8,128)(2,1)S(1)}, bf16[134,1024]{1,0:T(8,128)(2,1)S(1)}, u32[]{:S(2)}, u32[]{:S(2)}) collective-permute-start(bf16[134,1024]{1,0:T(8,128)(2,1)S(1)} %pad_maximum_fusion.1), channel_id=1, source_target_pairs={{0,4},{4,8},{8,12},{12,16},{16,20},{20,24},{24,28},{1,5},{5,9},{9,... | collective-permute-start | bytes 823304 | tf_op jit(solution)/shard_map/ppermute | solution.py:20
  212.1 9.1 %copy-start = (bf16[3,512,1024]{2,1,0:T(8,128)(2,1)S(1)}, bf16[3,512,1024]{2,1,0:T(8,128)(2,1)}, u32[]{:S(2)}) copy-start(bf16[3,512,1024]{2,1,0:T(8,128)(2,1)} %shard_map.73) | copy-start | bytes 9437188
  235.3 1.6 copy-start.1
  244.3 2.9 %copy-start.3 = (f32[1024]{0:T(1024)S(1)}, f32[1024]{0:T(1024)}, u32[]{:S(2)}) copy-start(f32[1024]{0:T(1024)} %param.13) | copy-start | bytes 12292
